TPU v7x, 32 devices: a whole 2x2x4 slice. The times are simulated.
32 devices in a mesh: row: 4 (over z), col: 8 (over y, x, core).
Axes of the slice: x: 2, y: 2, z: 4, core: 2. Of those that a mesh axis runs over, the one named last changes fastest.
Arguments:
- features: bfloat16 [6144, 512], P(('col', 'row')), may hold values from -6 to 6
- out_grad: bfloat16 [6144, 512], P(('row', 'col')), may hold values from -6 to 6
- weight: bfloat16 [512, 512], replicated, may hold values from -0.25 to 0.25
- block_values: bfloat16 [4, 8, 72, 4096], P('row', 'col'), may hold values from -0.25 to 0.25
- block_coords: int32 [4, 8, 2, 72], P('row', 'col'), may hold values from 0 to 23, as said below
- block_counts: int32 [4, 8], P('row', 'col'), may hold values from 1 to 72, as said below
Outputs:
- activations: bfloat16 [6144, 512], P(('row', 'col'))
- weight_grad: float32 [512, 512], replicated
- feature_grad: bfloat16 [6144, 512], P(('col', 'row'))
Inputs may be any that keep to these rules, and one draw needn't show every extreme that they name: `block_coords`: entry 0 of a slot is a block row below 24, entry 1 a block column below 12; the 72 slots of a tile name distinct blocks. `block_counts`: slots from the count onward are padding: their coordinates and values are ignored. Some tile has exactly 72 live slots.
All inputs are finite; a program needn't handle non-finite values.
Results may differ from a plain program's by a relative error of at most 0.025.
Values may be sent and summed in bfloat16 or wider, within the bound.
A program may use at most 128 MiB of HBM per device.

v0:
```python
import math

import jax
import jax.numpy as jnp
from jax import lax
from jax.sharding import PartitionSpec as P


def settle(term):
    return lax.optimization_barrier(term.astype(jnp.bfloat16)).astype(jnp.float32)


def per_device(features, out_grad, weight, block_values, block_coords, block_counts):
    row_devices = lax.axis_size("row")
    col_devices = lax.axis_size("col")
    node_count = features.shape[0]
    side = 64
    slot_total = block_values.shape[2]
    block_rows = node_count * col_devices // side
    block_cols = node_count * row_devices // side
    live_count = block_counts[0, 0]
    row_ids = block_coords[0, 0, 0]
    col_ids = block_coords[0, 0, 1]
    slot_vals = block_values.reshape(slot_total, side, side)
    live = jnp.arange(slot_total, dtype=jnp.int32) < live_count
    slot_vals = jnp.where(live[:, None, None], slot_vals, jnp.zeros_like(slot_vals))
    panel = lax.all_gather(features, "row", axis=0, tiled=True)
    dense_tile = jnp.zeros((block_rows, side, block_cols, side), jnp.bfloat16)
    dense_tile = dense_tile.at[row_ids, :, col_ids, :].add(slot_vals)
    dense_tile = dense_tile.reshape(block_rows * side, block_cols * side)
    partial_agg = settle(jnp.dot(dense_tile, panel, preferred_element_type=jnp.float32))
    aggregated = lax.psum_scatter(
        partial_agg.astype(jnp.bfloat16), "col", scatter_dimension=0, tiled=True
    )
    pre_act = jnp.dot(aggregated, weight, preferred_element_type=jnp.float32)
    sigmoid_pre = jax.nn.sigmoid(pre_act)
    activations = (pre_act * sigmoid_pre).astype(jnp.bfloat16)
    grad_pre = (
        out_grad.astype(jnp.float32) * sigmoid_pre * (1.0 + pre_act * (1.0 - sigmoid_pre))
    ).astype(jnp.bfloat16)
    activations, grad_pre = (activations, grad_pre)
    grad_agg = lax.dot_general(
        grad_pre, weight, (((1,), (1,)), ((), ())), preferred_element_type=jnp.float32
    ).astype(jnp.bfloat16)
    grad_rows = lax.all_gather(grad_agg, "col", axis=0, tiled=True)
    local_wgrad = lax.dot_general(
        aggregated, grad_pre, (((0,), (0,)), ((), ())), preferred_element_type=jnp.float32
    )
    total_nodes = node_count * row_devices * col_devices
    weight_grad = lax.psum(local_wgrad, ("row", "col")) * jnp.float32(1.0 / math.sqrt(total_nodes))
    partial_grad = settle(
        lax.dot_general(
            dense_tile, grad_rows, (((0,), (0,)), ((), ())), preferred_element_type=jnp.float32
        )
    )
    feature_grad = lax.psum_scatter(
        partial_grad.astype(jnp.bfloat16), "row", scatter_dimension=0, tiled=True
    )
    return (activations, weight_grad, feature_grad)


def solution(mesh):
    return jax.shard_map(
        per_device,
        mesh=mesh,
        in_specs=(
            P(("col", "row"), None),
            P(("row", "col"), None),
            P(),
            P("row", "col", None, None),
            P("row", "col", None, None),
            P("row", "col"),
        ),
        out_specs=(P(("row", "col"), None), P(), P(("col", "row"), None)),
        check_vma=False,
    )
```

profile of v0, /device:TPU:0, one launch (start us, length us, event | category | flops | bytes accessed | tf_op | source)
XLA Modules:
  0.0 297.9 jit_solution(656508431607916051)
XLA Ops:
  7.2 0.0 copy-start
  7.2 0.0 copy-start.4
  7.2 0.0 reduce-scatter.3.cloned.1.call-start
  7.2 2.2 reshape.72
  10.1 0.0 copy-done.4
  10.2 0.2 broadcast_select_fusion
  10.3 3.3 %broadcast_in_dim.17 = bf16[24,64,12,64]{3,1,2,0:T(8,128)(2,1)} broadcast(bf16[]{:T(256)} %constant.6.clone.1), dimensions={} | broadcast | bytes 2359298 | tf_op jit(solution)/shard_map/broadcast_in_dim | solution.py:28
  13.7 11.9 %scatter_fusion = bf16[24,64,12,64]{3,1,2,0:T(8,128)(2,1)} fusion(bf16[24,64,12,64]{3,1,2,0:T(8,128)(2,1)} %broadcast_in_dim.17, s32[72]{0:T(128)S(1)} %fusion.1, bf16[72,64,64]{2,1,0:T(8,128)(2,1)S(1)} %broadcast_select_fusion), kind=kCustom, calls=%fused_computation | custom fusion | flops 294912 | bytes 1770048 | tf_op jit(solution)/shard_map/scatter-add | solution.py:29
  25.6 7.0 %copy.9 = bf16[24,64,12,64]{1,0,3,2:T(8,128)(2,1)} copy(bf16[24,64,12,64]{3,1,2,0:T(8,128)(2,1)} %scatter_fusion) | data formatting | bytes 4718592 | tf_op jit(solution)/shard_map/scatter-add | solution.py:29
  32.6 6.2 %reshape.73 = bf16[1536,768]{0,1:T(8,128)(2,1)S(1)} reshape(bf16[24,64,12,64]{1,0,3,2:T(8,128)(2,1)} %copy.9) | data formatting | bytes 4718592 | tf_op jit(solution)/shard_map/reshape | solution.py:30
  38.8 0.0 copy-done.1
  38.9 21.3 %all_gather.6 = bf16[768,512]{1,0:T(8,128)(2,1)S(1)} all-gather(bf16[192,512]{1,0:T(8,128)(2,1)S(1)} %copy-done.1), channel_id=1, replica_groups=mesh['row'=4,'col'=8] {'row'}, dimensions={0}, use_global_device_ids=true | all-gather | bytes 983040 | tf_op jit(solution)/shard_map/all_gather | solution.py:27
  60.1 2.6 convolution_convert_fusion
  62.7 0.0 reduce-scatter.3.cloned.1.call-update
  62.7 0.0 copy-start.2
  62.7 0.0 all-gather.2.cloned.1.call-start
  62.8 38.3 %reduce-scatter.3.cloned.1.call-done = bf16[192,512]{1,0:T(8,128)(2,1)} async-done(((bf16[1536,512]{1,0:T(8,128)(2,1)}), bf16[192,512]{1,0:T(8,128)(2,1)}) %reduce-scatter.3.cloned.1.call-update) | async-done | bytes 196624 | tf_op jit(solution)/shard_map/reduce_scatter | solution.py:32
  101.1 1.9 multiply_convert_fusion.1
  103.0 0.8 copy-done.5
  103.8 0.0 copy-done.2
  103.8 1.0 convolution_convert_fusion.2
  104.8 0.0 all-gather.2.cloned.1.call-update
  104.8 0.0 all-reduce.2.cloned.1.call-start
  104.9 2.4 fusion.2
  107.3 0.0 all-reduce.2.cloned.1.call-update
  107.3 0.0 reduce-scatter.5.cloned.1.call-start
  107.3 23.3 %all-gather.2.cloned.1.call-done = bf16[1536,512]{1,0:T(8,128)(2,1)} async-done(((bf16[192,512]{1,0:T(8,128)(2,1)}), bf16[1536,512]{1,0:T(8,128)(2,1)}) %all-gather.2.cloned.1.call-update) | async-done | bytes 1572880 | tf_op jit(solution)/shard_map/all_gather | solution.py:45
  130.7 3.7 %convolution_convert_fusion.1 = bf16[768,512]{1,0:T(8,128)(2,1)} fusion(bf16[1536,768]{0,1:T(8,128)(2,1)S(1)} %reshape.73, bf16[1536,512]{1,0:T(8,128)(2,1)} %all-gather.2.cloned.1.call-done), kind=kOutput, calls=%fused_computation.2 | convolution fusion | flops 1208352768 | bytes 4718592 | tf_op jit(solution)/shard_map/dot_general | solution.py:52
  134.3 0.0 reduce-scatter.5.cloned.1.call-update
  134.4 131.9 %all-reduce.2.cloned.1.call-done = f32[512,512]{1,0:T(8,128)} async-done(((f32[512,512]{1,0:T(8,128)}), f32[512,512]{1,0:T(8,128)}) %all-reduce.2.cloned.1.call-update) | async-done | bytes 1048592 | tf_op jit(solution)/shard_map/psum | solution.py:50
  266.2 2.3 broadcast_multiply_fusion
  268.5 22.8 %reduce-scatter.5.cloned.1.call-done = bf16[192,512]{1,0:T(8,128)(2,1)} async-done(((bf16[768,512]{1,0:T(8,128)(2,1)}), bf16[192,512]{1,0:T(8,128)(2,1)}) %reduce-scatter.5.cloned.1.call-update) | async-done | bytes 196624 | tf_op jit(solution)/shard_map/reduce_scatter | solution.py:56
  (7 shorter events, 0.0 us)
Async XLA Ops:
  7.2 93.9 %copy-start = (bf16[512,512]{1,0:T(8,128)(2,1)S(1)}, bf16[512,512]{1,0:T(8,128)(2,1)}, u32[]{:S(2)}) copy-start(bf16[512,512]{1,0:T(8,128)(2,1)} %param.8) | copy-start | bytes 1572868
  7.2 3.0 copy-start.4
  7.2 93.9 %reduce-scatter.3.cloned.1.call-start = ((), (), s32[]{:S(2)}) async-start(), calls=%async_computation.2 | async-start | bytes 1769472 | tf_op jit(solution)/shard_map/reduce_scatter | solution.py:32
  32.6 6.2 %copy-start.1 = (bf16[192,512]{1,0:T(8,128)(2,1)S(1)}, bf16[192,512]{1,0:T(8,128)(2,1)}, u32[]{:S(2)}) copy-start(bf16[192,512]{1,0:T(8,128)(2,1)} %param.6) | copy-start | bytes 589828
  62.7 41.0 %copy-start.2 = (bf16[192,512]{1,0:T(8,128)(2,1)S(1)}, bf16[192,512]{1,0:T(8,128)(2,1)}, u32[]{:S(2)}) copy-start(bf16[192,512]{1,0:T(8,128)(2,1)} %param.7) | copy-start | bytes 589828
  62.7 67.9 %all-gather.2.cloned.1.call-start = ((), (), s32[]{:S(2)}) async-start(), calls=%async_computation.4 | async-start | bytes 1769472 | tf_op jit(solution)/shard_map/all_gather | solution.py:45
  103.0 0.8 copy-start.5
  103.0 1.9 copy-start.3
  104.8 161.4 %all-reduce.2.cloned.1.call-start = ((), (), s32[]{:S(2)}) async-start(), calls=%async_computation.3 | async-start | bytes 2097152 | tf_op jit(solution)/shard_map/psum | solution.py:50
  107.3 184.0 %reduce-scatter.5.cloned.1.call-start = ((), (), s32[]{:S(2)}) async-start(), calls=%async_computation.5 | async-start | bytes 983040 | tf_op jit(solution)/shard_map/reduce_scatter | solution.py:56
Sparse Core Ops, SparseCore 0:
  62.8 38.1 reduce-scatter.2
  104.9 25.6 all-gather.1
  136.4 129.7 all-reduce.1
  269.0 22.2 reduce-scatter.4
where the time goes:
time: 299 us; the launch traced here: 298 us
  waiting for transfers between devices  216 us (72%)
  blocking collectives  21.3 us (7%)
  local copies, waits for them, and re-layouts  19.6 us (7%)
  between operations  14.5 us (5%)
  other arithmetic  14.4 us (5%)
  matrix products  11.6 us (4%)
    psum x1, waiting for transfers between devices, per_device(): lax.psum(local_wgrad, ('row', 'col'))  132 us
    reduce_scatter x1, waiting for transfers between devices, per_device(): lax.psum_scatter(partial_agg.astype(jnp.bfloat16), 'col', scatter_dimensi...  38.3 us
    all_gather x1, waiting for transfers between devices, per_device(): grad_rows = lax.all_gather(grad_agg, 'col', axis=0, tiled=True)  23.3 us
    reduce_scatter x1, waiting for transfers between devices, per_device(): lax.psum_scatter(partial_grad.astype(jnp.bfloat16), 'row', scatter_dimens...  22.8 us
    all_gather x1, blocking collectives, per_device(): panel = lax.all_gather(features, 'row', axis=0, tiled=True)  21.3 us
    scatter-add x1, other arithmetic, per_device(): dense_tile = dense_tile.at[row_ids, :, col_ids, :].add(slot_vals)  11.9 us
    scatter-add x1, local copies, waits for them, and re-layouts, per_device(): dense_tile = dense_tile.at[row_ids, :, col_ids, :].add(slot_vals)  7.03 us
    reshape x1, local copies, waits for them, and re-layouts, per_device(): dense_tile = dense_tile.reshape(block_rows * side, block_cols * side)  6.19 us
  transfers between devices with their start and end apart: 4, of which 4 were waited for; matrix products, arithmetic and copies ran while one was open for 3% of the time, Pallas kernels for 0%

commit v1 on v0

v1 whole, which is shorter than its diff:
```python
import functools
import math

import jax
import jax.numpy as jnp
from jax import lax
from jax.experimental import pallas as pl
from jax.experimental.pallas import tpu as pltpu
from jax.sharding import PartitionSpec as P

SIDE = 64
CHUNKS = 2
F32 = jnp.float32
BF16 = jnp.bfloat16


def kernel(
    R, C, scale,
    slot_ref, feat_ref, og_ref, w_ref, vals_ref,
    act_ref, wgrad_ref, fgrad_ref,
    dense, dense_t, panel, own, a_send, a_recv, b_send, b_recv, agg_ref, gpre_ref,
    gfull, f_send, f_recv, wg, wa_send, wa_recv, wb_send, wb_recv, wz, wfull,
    feat_ss, feat_rs, a_ss, a_rs, b_ss, b_rs, g_ss, g_rs, gs_ss, gs_rs, f_ss, f_rs,
    wa_ss, wa_rs, wb_ss, wb_rs, wz_ss, wz_rs, wh_ss, wh_rs, ws_ss, ws_rs,
):
    K = CHUNKS
    rows, width = feat_ref.shape
    dc = width // K
    NC = C // 2
    r = lax.axis_index("row")
    c = lax.axis_index("col")
    chip = c // 2
    core = c % 2
    other = 1 - core
    sib = 2 * chip + other
    brows = rows * C // SIDE
    bcols = rows * R // SIDE

    def row_peer(d):
        return (r + d) % R

    def chip_peer(d):
        return 2 * ((chip + d) % NC) + core

    def remote(src, dst, ss, rs, axis, peer):
        return pltpu.make_async_remote_copy(
            src_ref=src, dst_ref=dst, send_sem=ss, recv_sem=rs,
            device_id={axis: peer}, device_id_type=pl.DeviceIdType.MESH,
        )

    barrier = pltpu.get_barrier_semaphore()
    for d in range(1, R):
        pl.semaphore_signal(barrier, inc=1, device_id={"row": row_peer(d)},
                            device_id_type=pl.DeviceIdType.MESH)
    for d in range(1, NC):
        pl.semaphore_signal(barrier, inc=1, device_id={"col": chip_peer(d)},
                            device_id_type=pl.DeviceIdType.MESH)
    pl.semaphore_signal(barrier, inc=1, device_id={"col": sib},
                        device_id_type=pl.DeviceIdType.MESH)
    pl.semaphore_wait(barrier, R - 1 + NC - 1 + 1)

    sends = []

    def go(copy):
        copy.start()
        sends.append(copy)
        return copy

    feat = {}
    for k in range(K):
        for d in range(R - 1, 0, -1):
            feat[k, d] = go(remote(
                feat_ref.at[:, pl.ds(k * dc, dc)], panel.at[k, r],
                feat_ss.at[k, d], feat_rs.at[k, d], "row", row_peer(d)))
    for k in range(K):
        panel[k, r] = feat_ref[:, k * dc:(k + 1) * dc]

    @pl.loop(0, brows)
    def _(br):
        for p in range(bcols // 2):
            halves = []
            for h in range(2):
                slot = slot_ref[br * bcols + 2 * p + h]
                live = jnp.where(slot >= 0, 1.0, 0.0).astype(F32)
                block = vals_ref[jnp.maximum(slot, 0)]
                halves.append(block.astype(F32) * live)
            pair = jnp.concatenate(halves, axis=1).astype(BF16)
            dense[pl.ds(pl.multiple_of(br * SIDE, SIDE), SIDE), p * 128:(p + 1) * 128] = pair

    @pl.loop(0, brows * SIDE // 128)
    def _(i):
        at = pl.ds(pl.multiple_of(i * 128, 128), 128)
        dense_t[:, at] = dense[at, :].astype(F32).T.astype(BF16)

    ab = {}
    for k in range(K):
        for d in range(1, R):
            feat[k, d].wait_recv()

        def product(piece):
            at = pl.ds(pl.multiple_of(piece * rows, 64), rows)
            return jnp.dot(dense[at, :], panel[k].reshape(R * rows, dc),
                           preferred_element_type=F32)

        @pl.loop(0, NC)
        def _(q):
            a_send[k, q] = product(2 * q + other).astype(BF16)

        a_copy = go(remote(a_send.at[k], a_recv.at[k], a_ss.at[k], a_rs.at[k], "col", sib))

        @pl.loop(0, NC)
        def _(q):
            own[q] = product(2 * q + core)

        a_copy.wait_recv()
        for d in range(NC - 1, -1, -1):
            q = (chip + d) % NC
            total = own[q] + a_recv[k, q].astype(F32)
            if d == 0:
                own[q] = total
                agg_ref[:, k * dc:(k + 1) * dc] = total
            else:
                b_send[k, q] = total.astype(BF16)
                ab[k, d] = go(remote(b_send.at[k, q], b_recv.at[k, d],
                                     b_ss.at[k, d], b_rs.at[k, d], "col", chip_peer(d)))
    for k in range(K):
        total = agg_ref[:, k * dc:(k + 1) * dc]
        for d in range(1, NC):
            ab[k, d].wait_recv()
            total = total + b_recv[k, d].astype(F32)
        agg_ref[:, k * dc:(k + 1) * dc] = total

    agg = agg_ref[...].astype(BF16)
    pre = jnp.dot(agg, w_ref[...], preferred_element_type=F32)
    sig = jax.nn.sigmoid(pre)
    act_ref[...] = (pre * sig).astype(BF16)
    gpre_ref[...] = (og_ref[...].astype(F32) * sig * (1.0 + pre * (1.0 - sig))).astype(BF16)

    hop, direct = {}, {}
    for k in range(K):
        gfull[k, c] = lax.dot_general(
            gpre_ref[...], w_ref[k * dc:(k + 1) * dc, :], (((1,), (1,)), ((), ())),
            preferred_element_type=F32).astype(BF16)
        for d in range(NC - 1, 0, -1):
            direct[k, d] = go(remote(gfull.at[k, c], gfull.at[k, c],
                                     g_ss.at[k, d], g_rs.at[k, d], "col", chip_peer(d)))
        hop[k, 0] = go(remote(gfull.at[k, c], gfull.at[k, c],
                              gs_ss.at[k, 0], gs_rs.at[k, 0], "col", sib))

    part = width // C
    local = jnp.dot(agg_ref[...].T.astype(BF16), gpre_ref[...], preferred_element_type=F32)
    wg[...] = local.reshape(C, part, width)
    for q in range(NC):
        wa_send[q] = wg[2 * q + other].astype(BF16)
    wa = go(remote(wa_send, wa_recv, wa_ss, wa_rs, "col", sib))
    wa.wait_recv()
    wb = {}
    for d in range(1, NC):
        q = (chip + d) % NC
        wb_send[q] = (wg[2 * q + core] + wa_recv[q].astype(F32)).astype(BF16)
        wb[d] = go(remote(wb_send.at[q], wb_recv.at[d], wb_ss.at[d], wb_rs.at[d],
                          "col", chip_peer(d)))

    fr, wzc = {}, {}
    for k in range(K):
        for d in range(1, NC):
            direct[k, d].wait_recv()
            src = 2 * ((chip + NC - d) % NC) + core
            hop[k, d] = go(remote(gfull.at[k, src], gfull.at[k, src],
                                  gs_ss.at[k, d], gs_rs.at[k, d], "col", sib))
        for d in range(NC):
            hop[k, d].wait_recv()

        def back(piece):
            at = pl.ds(pl.multiple_of(piece * rows, 64), rows)
            return jnp.dot(dense_t[at, :], gfull[k].reshape(C * rows, dc),
                           preferred_element_type=F32)

        for d in range(R - 1, -1, -1):
            t = row_peer(d)
            if d:
                f_send[k, d] = back(t).astype(BF16)
                fr[k, d] = go(remote(f_send.at[k, d], f_recv.at[k, d],
                                     f_ss.at[k, d], f_rs.at[k, d], "row", t))
            else:
                own[k] = back(t)

        if k == 0:
            total = wg[c] + wa_recv[chip].astype(F32)
            for d in range(1, NC):
                wb[d].wait_recv()
                total = total + wb_recv[d].astype(F32)
            wz[r] = total.astype(BF16)
            for d in range(R - 1, 0, -1):
                wzc[d] = go(remote(wz.at[r], wz.at[r], wz_ss.at[d], wz_rs.at[d],
                                   "row", row_peer(d)))

    for d in range(1, R):
        wzc[d].wait_recv()
    total = wz[0].astype(F32)
    for i in range(1, R):
        total = total + wz[i].astype(F32)
    wfull[c] = total.astype(BF16)
    wd, wh = {}, {}
    for d in range(NC - 1, 0, -1):
        wd[d] = go(remote(wfull.at[c], wfull.at[c], wh_ss.at[d], wh_rs.at[d],
                          "col", chip_peer(d)))
    wh[0] = go(remote(wfull.at[c], wfull.at[c], ws_ss.at[0], ws_rs.at[0], "col", sib))
    for d in range(1, NC):
        wd[d].wait_recv()
        src = 2 * ((chip + NC - d) % NC) + core
        wh[d] = go(remote(wfull.at[src], wfull.at[src], ws_ss.at[d], ws_rs.at[d], "col", sib))
    for d in range(NC):
        wh[d].wait_recv()
    for i in range(C):
        wgrad_ref[i * part:(i + 1) * part, :] = wfull[i].astype(F32) * scale

    for k in range(K):
        total = own[k]
        for d in range(1, R):
            fr[k, d].wait_recv()
            total = total + f_recv[k, d].astype(F32)
        fgrad_ref[:, k * dc:(k + 1) * dc] = total.astype(BF16)

    for copy in sends:
        copy.wait_send()


def per_device(features, out_grad, weight, block_values, block_coords, block_counts):
    R = lax.axis_size("row")
    C = lax.axis_size("col")
    rows, width = features.shape
    slots = block_values.shape[2]
    brows = rows * C // SIDE
    bcols = rows * R // SIDE
    NC = C // 2
    K = CHUNKS
    dc = width // K
    part = width // C
    ids = jnp.arange(slots, dtype=jnp.int32)
    place = block_coords[0, 0, 0] * bcols + block_coords[0, 0, 1]
    place = jnp.where(ids < block_counts[0, 0], place, -1)
    at = jnp.arange(brows * bcols, dtype=jnp.int32)
    slot_of = jnp.max(jnp.where(place[None, :] == at[:, None], ids[None, :], -1), axis=1)
    vals = block_values.reshape(slots, SIDE, SIDE)
    scale = 1.0 / math.sqrt(rows * R * C)
    vmem = pl.BlockSpec(memory_space=pltpu.VMEM)
    dma = pltpu.SemaphoreType.DMA
    return pl.pallas_call(
        functools.partial(kernel, R, C, scale),
        out_shape=(
            jax.ShapeDtypeStruct((rows, width), BF16),
            jax.ShapeDtypeStruct((width, width), F32),
            jax.ShapeDtypeStruct((rows, width), BF16),
        ),
        in_specs=[pl.BlockSpec(memory_space=pltpu.SMEM), vmem, vmem, vmem, vmem],
        out_specs=(vmem, vmem, vmem),
        scratch_shapes=[
            pltpu.VMEM((brows * SIDE, bcols * SIDE), BF16),
            pltpu.VMEM((bcols * SIDE, brows * SIDE), BF16),
            pltpu.VMEM((K, R, rows, dc), BF16),
            pltpu.VMEM((NC, rows, dc), F32),
            pltpu.VMEM((K, NC, rows, dc), BF16),
            pltpu.VMEM((K, NC, rows, dc), BF16),
            pltpu.VMEM((K, NC, rows, dc), BF16),
            pltpu.VMEM((K, NC, rows, dc), BF16),
            pltpu.VMEM((rows, width), F32),
            pltpu.VMEM((rows, width), BF16),
            pltpu.VMEM((K, C, rows, dc), BF16),
            pltpu.VMEM((K, R, rows, dc), BF16),
            pltpu.VMEM((K, R, rows, dc), BF16),
            pltpu.VMEM((C, part, width), F32),
            pltpu.VMEM((NC, part, width), BF16),
            pltpu.VMEM((NC, part, width), BF16),
            pltpu.VMEM((NC, part, width), BF16),
            pltpu.VMEM((NC, part, width), BF16),
            pltpu.VMEM((R, part, width), BF16),
            pltpu.VMEM((C, part, width), BF16),
            dma((K, R)), dma((K, R)),
            dma((K,)), dma((K,)),
            dma((K, NC)), dma((K, NC)),
            dma((K, NC)), dma((K, NC)),
            dma((K, NC)), dma((K, NC)),
            dma((K, R)), dma((K, R)),
            dma, dma,
            dma((NC,)), dma((NC,)),
            dma((R,)), dma((R,)),
            dma((NC,)), dma((NC,)),
            dma((NC,)), dma((NC,)),
        ],
        compiler_params=pltpu.CompilerParams(
            collective_id=0, has_side_effects=True, vmem_limit_bytes=60 * 1024 * 1024
        ),
    )(slot_of, features, out_grad, weight, vals)


def solution(mesh):
    return jax.shard_map(
        per_device,
        mesh=mesh,
        in_specs=(
            P(("col", "row"), None),
            P(("row", "col"), None),
            P(),
            P("row", "col", None, None),
            P("row", "col", None, None),
            P("row", "col"),
        ),
        out_specs=(P(("row", "col"), None), P(), P(("col", "row"), None)),
        check_vma=False,
    )
```

time: 299 us -> 83.8 us (0.28)
  waiting for transfers between devices: 216 us -> 0 us
  Pallas kernels: 0 us -> 73.3 us
  blocking collectives: 21.3 us -> 0 us
  between operations: 14.5 us -> 1.3 us
  other arithmetic: 14.4 us -> 1.44 us
  local copies, waits for them, and re-layouts: 19.6 us -> 7.53 us
  matrix products: 11.6 us -> 0 us
    psum x1 -> x0, waiting for transfers between devices: 132 us -> none  [per_device(): lax.psum(local_wgrad, ('row', 'col'))]
    pallas_call x0 -> x1, Pallas kernels: none -> 73.3 us  [per_device(): pl.pallas_call(functools.partial(kernel, R, C, scale), out_shape=(jax.Sha...]
    reduce_scatter x2 -> x0, waiting for transfers between devices: 61.1 us -> none  [the longest x1 38.3 us: per_device(): lax.psum_scatter(partial_agg.astype(jnp.bfloat16), 'col', scatter_dimensi...]
    all_gather x1 -> x0, waiting for transfers between devices: 23.3 us -> none  [per_device(): grad_rows = lax.all_gather(grad_agg, 'col', axis=0, tiled=True)]
    all_gather x1 -> x0, blocking collectives: 21.3 us -> none  [per_device(): panel = lax.all_gather(features, 'row', axis=0, tiled=True)]
    scatter-add x1 -> x0, other arithmetic: 11.9 us -> none  [per_device(): dense_tile = dense_tile.at[row_ids, :, col_ids, :].add(slot_vals)]
    dot_general x5 -> x0, matrix products: 11.6 us -> none  [the longest x1 3.68 us: per_device(): lax.dot_general(dense_tile, grad_rows, (((0,), (0,)), ((), ())), preferre...]
    scatter-add x1 -> x0, local copies, waits for them, and re-layouts: 7.03 us -> none  [per_device(): dense_tile = dense_tile.at[row_ids, :, col_ids, :].add(slot_vals)]
  transfers between devices with their start and end apart: 4 -> 0, of which waited for: 4 -> 0; matrix products, arithmetic and copies ran while one was open for 3% -> 0% of each run, Pallas kernels for 0% -> 0%
where the time goes in v1:
time: 83.8 us; the launch traced here: 83.6 us
  Pallas kernels  73.3 us (87%)
  local copies, waits for them, and re-layouts  7.53 us (9%)
  other arithmetic  1.44 us (2%)
  between operations  1.3 us (2%)
    pallas_call x1, Pallas kernels, per_device(): pl.pallas_call(functools.partial(kernel, R, C, scale), out_shape=(jax.Sha...  73.3 us
    unnamed x5, local copies, waits for them, and re-layouts  4.6 us
    reshape x1, local copies, waits for them, and re-layouts, per_device(): vals = block_values.reshape(slots, SIDE, SIDE)  2.93 us

profile of v1, /device:TPU:0, one launch (start us, length us, event | category | flops | bytes accessed | tf_op | source)
XLA Modules:
  0.0 83.6 jit_solution(7735565778138077457)
XLA Ops:
  1.3 0.8 compare_select_fusion
  2.0 0.7 select_reduce_fusion.slot_ref
  2.7 2.9 %reshape.27.vals_ref = bf16[72,64,64]{2,1,0:T(8,128)(2,1)} reshape(bf16[1,1,72,4096]{3,2,1,0:T(8,128)(2,1)} %param.9) | data formatting | bytes 1179648 | tf_op jit(solution)/shard_map/reshape | solution.py:245
  5.6 73.3 %shard_map.85 = (bf16[192,512]{1,0:T(8,128)(2,1)}, f32[512,512]{1,0:T(8,128)}, bf16[192,512]{1,0:T(8,128)(2,1)}) custom-call(s32[288]{0:T(512)} %select_reduce_fusion.slot_ref, bf16[192,512]{1,0:T(8,128)(2,1)} %feat_ref.1, bf16[192,512]{1,0:T(8,128)(2,1)} %og_ref.1, bf16[512,512]{1,0:T(8,128)(2,1)} %w_ref.1, bf16[72,64,64]{2,1,0:T(8,128)(2,1)} %reshape.27.vals_ref), custom_call_target="tpu_custom_call" | custom-call | tf_op jit(solution)/shard_map/pallas_call | solution.py:249
  79.0 0.0 copy-start
  79.0 1.7 %copy.13 = bf16[192,512]{1,0:T(8,128)(2,1)} copy(bf16[192,512]{1,0:T(8,128)(2,1)} %get-tuple-element.6) | data formatting | bytes 393216
  80.6 2.3 %copy.14 = f32[512,512]{1,0:T(8,128)} copy(f32[512,512]{1,0:T(8,128)} %get-tuple-element.7) | data formatting | bytes 2097152
  82.9 0.0 copy-done
  82.9 0.7 copy.15
Async XLA Ops:
  79.0 3.9 %copy-start = (bf16[192,512]{1,0:T(8,128)(2,1)S(1)}, bf16[192,512]{1,0:T(8,128)(2,1)}, u32[]{:S(2)}) copy-start(bf16[192,512]{1,0:T(8,128)(2,1)} %get-tuple-element.8) | copy-start | bytes 589828

commit v2 on v1

--- a/solution.py
+++ b/solution.py
@@ -9,17 +9,17 @@
 from jax.sharding import PartitionSpec as P
 
 SIDE = 64
-CHUNKS = 2
+CHUNKS = 4
 F32 = jnp.float32
 BF16 = jnp.bfloat16
 
 
 def kernel(
-    R, C, scale,
+    R, C,
     slot_ref, feat_ref, og_ref, w_ref, vals_ref,
     act_ref, wgrad_ref, fgrad_ref,
     dense, dense_t, panel, own, a_send, a_recv, b_send, b_recv, agg_ref, gpre_ref,
-    gfull, f_send, f_recv, wg, wa_send, wa_recv, wb_send, wb_recv, wz, wfull,
+    gfull, f_own, f_total, f_send, f_recv, wg, wa_send, wa_recv, wb_send, wb_recv, wz, wfull,
     feat_ss, feat_rs, a_ss, a_rs, b_ss, b_rs, g_ss, g_rs, gs_ss, gs_rs, f_ss, f_rs,
     wa_ss, wa_rs, wb_ss, wb_rs, wz_ss, wz_rs, wh_ss, wh_rs, ws_ss, ws_rs,
 ):
@@ -63,15 +63,51 @@
 
     def go(copy):
         copy.start()
-        sends.append(copy)
+        sends.append((None, copy))
         return copy
 
-    feat = {}
-    for k in range(K):
-        for d in range(R - 1, 0, -1):
-            feat[k, d] = go(remote(
-                feat_ref.at[:, pl.ds(k * dc, dc)], panel.at[k, r],
-                feat_ss.at[k, d], feat_rs.at[k, d], "row", row_peer(d)))
+    def go_if(cond, copy):
+        @pl.when(cond)
+        def _():
+            copy.start()
+        sends.append((cond, copy))
+        return copy
+
+    def wait_if(cond, copy):
+        @pl.when(cond)
+        def _():
+            copy.wait_recv()
+
+    right, left = (r + 1) % R, (r + R - 1) % R
+
+    def feature_send(k, s):
+        for way in range(2):
+            if way == 0:
+                cond, origin, peer = (r < R - 1) & (r - s + 1 >= 0), (r + R - s + 1) % R, right
+            else:
+                cond, origin, peer = (r > 0) & (r + s - 1 <= R - 1), (r + s - 1) % R, left
+            src = feat_ref.at[:, pl.ds(k * dc, dc)] if s == 1 else panel.at[k, origin]
+            go_if(cond, remote(src, panel.at[k, origin], feat_ss.at[way, k, s],
+                               feat_rs.at[way, k, s], "row", peer))
+
+    def feature_wait(k, s):
+        for way in range(2):
+            if way == 0:
+                cond, origin, peer = r - s >= 0, (r + R - s) % R, left
+            else:
+                cond, origin, peer = r + s <= R - 1, (r + s) % R, right
+            wait_if(cond, remote(panel.at[k, origin], panel.at[k, origin],
+                                 feat_ss.at[way, k, s], feat_rs.at[way, k, s], "row", peer))
+
+    def feature_diagonal(t):
+        for k in range(K):
+            s = t - k
+            if 2 <= s <= R:
+                feature_wait(k, s - 1)
+            if 1 <= s <= R - 1:
+                feature_send(k, s)
+
+    feature_diagonal(1)
     for k in range(K):
         panel[k, r] = feat_ref[:, k * dc:(k + 1) * dc]
 
@@ -92,37 +128,42 @@
         at = pl.ds(pl.multiple_of(i * 128, 128), 128)
         dense_t[:, at] = dense[at, :].astype(F32).T.astype(BF16)
 
-    ab = {}
-    for k in range(K):
-        for d in range(1, R):
-            feat[k, d].wait_recv()
-
-        def product(piece):
-            at = pl.ds(pl.multiple_of(piece * rows, 64), rows)
-            return jnp.dot(dense[at, :], panel[k].reshape(R * rows, dc),
-                           preferred_element_type=F32)
-
-        @pl.loop(0, NC)
-        def _(q):
-            a_send[k, q] = product(2 * q + other).astype(BF16)
-
-        a_copy = go(remote(a_send.at[k], a_recv.at[k], a_ss.at[k], a_rs.at[k], "col", sib))
-
-        @pl.loop(0, NC)
-        def _(q):
-            own[q] = product(2 * q + core)
-
-        a_copy.wait_recv()
+    ab, pair_copy = {}, {}
+
+    def product(k, piece):
+        at = pl.ds(pl.multiple_of(piece * rows, 64), rows)
+        return jnp.dot(dense[at, :], panel[k].reshape(R * rows, dc),
+                       preferred_element_type=F32)
+
+    def pair_sum(k):
+        pair_copy[k].wait_recv()
         for d in range(NC - 1, -1, -1):
             q = (chip + d) % NC
             total = own[q] + a_recv[k, q].astype(F32)
             if d == 0:
-                own[q] = total
                 agg_ref[:, k * dc:(k + 1) * dc] = total
             else:
                 b_send[k, q] = total.astype(BF16)
                 ab[k, d] = go(remote(b_send.at[k, q], b_recv.at[k, d],
                                      b_ss.at[k, d], b_rs.at[k, d], "col", chip_peer(d)))
+
+    for t in range(2, R + K):
+        feature_diagonal(t)
+        k = t - R
+        if k >= 0:
+            @pl.loop(0, NC)
+            def _(q):
+                a_send[k, q] = product(k, 2 * q + other).astype(BF16)
+
+            pair_copy[k] = go(remote(a_send.at[k], a_recv.at[k], a_ss.at[k], a_rs.at[k],
+                                     "col", sib))
+            if k > 0:
+                pair_sum(k - 1)
+
+            @pl.loop(0, NC)
+            def _(q):
+                own[q] = product(k, 2 * q + core)
+    pair_sum(K - 1)
     for k in range(K):
         total = agg_ref[:, k * dc:(k + 1) * dc]
         for d in range(1, NC):
@@ -136,7 +177,8 @@
     act_ref[...] = (pre * sig).astype(BF16)
     gpre_ref[...] = (og_ref[...].astype(F32) * sig * (1.0 + pre * (1.0 - sig))).astype(BF16)
 
-    hop, direct = {}, {}
+    hop, direct, wb = {}, {}, {}
+    part = width // C
     for k in range(K):
         gfull[k, c] = lax.dot_general(
             gpre_ref[...], w_ref[k * dc:(k + 1) * dc, :], (((1,), (1,)), ((), ())),
@@ -146,46 +188,64 @@
                                      g_ss.at[k, d], g_rs.at[k, d], "col", chip_peer(d)))
         hop[k, 0] = go(remote(gfull.at[k, c], gfull.at[k, c],
                               gs_ss.at[k, 0], gs_rs.at[k, 0], "col", sib))
-
-    part = width // C
-    local = jnp.dot(agg_ref[...].T.astype(BF16), gpre_ref[...], preferred_element_type=F32)
-    wg[...] = local.reshape(C, part, width)
-    for q in range(NC):
-        wa_send[q] = wg[2 * q + other].astype(BF16)
-    wa = go(remote(wa_send, wa_recv, wa_ss, wa_rs, "col", sib))
-    wa.wait_recv()
-    wb = {}
-    for d in range(1, NC):
-        q = (chip + d) % NC
-        wb_send[q] = (wg[2 * q + core] + wa_recv[q].astype(F32)).astype(BF16)
-        wb[d] = go(remote(wb_send.at[q], wb_recv.at[d], wb_ss.at[d], wb_rs.at[d],
-                          "col", chip_peer(d)))
-
-    fr, wzc = {}, {}
-    for k in range(K):
-        for d in range(1, NC):
-            direct[k, d].wait_recv()
-            src = 2 * ((chip + NC - d) % NC) + core
-            hop[k, d] = go(remote(gfull.at[k, src], gfull.at[k, src],
-                                  gs_ss.at[k, d], gs_rs.at[k, d], "col", sib))
-        for d in range(NC):
-            hop[k, d].wait_recv()
-
-        def back(piece):
-            at = pl.ds(pl.multiple_of(piece * rows, 64), rows)
-            return jnp.dot(dense_t[at, :], gfull[k].reshape(C * rows, dc),
-                           preferred_element_type=F32)
-
-        for d in range(R - 1, -1, -1):
-            t = row_peer(d)
-            if d:
-                f_send[k, d] = back(t).astype(BF16)
-                fr[k, d] = go(remote(f_send.at[k, d], f_recv.at[k, d],
-                                     f_ss.at[k, d], f_rs.at[k, d], "row", t))
-            else:
-                own[k] = back(t)
-
-        if k == 0:
+        if k == 1:
+            local = jnp.dot(agg_ref[...].T.astype(BF16), gpre_ref[...],
+                            preferred_element_type=F32)
+            wg[...] = local.reshape(C, part, width)
+            for q in range(NC):
+                wa_send[q] = wg[2 * q + other].astype(BF16)
+            wa = go(remote(wa_send, wa_recv, wa_ss, wa_rs, "col", sib))
+        if k == 2:
+            wa.wait_recv()
+            for d in range(1, NC):
+                q = (chip + d) % NC
+                wb_send[q] = (wg[2 * q + core] + wa_recv[q].astype(F32)).astype(BF16)
+                wb[d] = go(remote(wb_send.at[q], wb_recv.at[d], wb_ss.at[d], wb_rs.at[d],
+                                  "col", chip_peer(d)))
+
+    wzc = {}
+
+    def tail_copy(way, k, t, peer):
+        return remote(f_send.at[way, k, t], f_recv.at[way, k, t],
+                      f_ss.at[way, k, t], f_rs.at[way, k, t], "row", peer)
+
+    def tail_send(k, s, way):
+        at_r = s if way == 0 else R - 1 - s
+        targets = range(R - 1, at_r, -1) if way == 0 else range(0, at_r)
+
+        @pl.when(r == at_r)
+        def _():
+            for t in targets:
+                total = f_own[k, t]
+                if s:
+                    tail_copy(way, k, t, left if way == 0 else right).wait_recv()
+                    total = total + f_recv[way, k, t].astype(F32)
+                f_send[way, k, t] = total.astype(BF16)
+                tail_copy(way, k, t, right if way == 0 else left).start()
+
+    for tau in range(K + R - 2):
+        if tau < K:
+            k = tau
+            for d in range(1, NC):
+                direct[k, d].wait_recv()
+                src = 2 * ((chip + NC - d) % NC) + core
+                hop[k, d] = go(remote(gfull.at[k, src], gfull.at[k, src],
+                                      gs_ss.at[k, d], gs_rs.at[k, d], "col", sib))
+            for d in range(NC):
+                hop[k, d].wait_recv()
+
+            @pl.loop(0, R)
+            def _(t):
+                at = pl.ds(pl.multiple_of(t * rows, 64), rows)
+                f_own[k, t] = jnp.dot(dense_t[at, :], gfull[k].reshape(C * rows, dc),
+                                      preferred_element_type=F32)
+
+        for s in range(R - 1):
+            if 0 <= tau - s < K:
+                tail_send(tau - s, s, 0)
+                tail_send(tau - s, s, 1)
+
+        if tau == 2:
             total = wg[c] + wa_recv[chip].astype(F32)
             for d in range(1, NC):
                 wb[d].wait_recv()
@@ -213,17 +273,33 @@
     for d in range(NC):
         wh[d].wait_recv()
     for i in range(C):
-        wgrad_ref[i * part:(i + 1) * part, :] = wfull[i].astype(F32) * scale
-
-    for k in range(K):
-        total = own[k]
-        for d in range(1, R):
-            fr[k, d].wait_recv()
-            total = total + f_recv[k, d].astype(F32)
-        fgrad_ref[:, k * dc:(k + 1) * dc] = total.astype(BF16)
-
-    for copy in sends:
-        copy.wait_send()
+        wgrad_ref[i * part:(i + 1) * part, :] = wfull[i]
+
+    for k in range(K):
+        f_total[...] = f_own[k, r]
+        for way in range(2):
+            @pl.when(r > 0 if way == 0 else r < R - 1)
+            def _():
+                tail_copy(way, k, r, left if way == 0 else right).wait_recv()
+                f_total[...] += f_recv[way, k, r].astype(F32)
+        fgrad_ref[:, k * dc:(k + 1) * dc] = f_total[...].astype(BF16)
+
+    for k in range(K):
+        for t in range(R):
+            @pl.when(r < t)
+            def _():
+                tail_copy(0, k, t, right).wait_send()
+
+            @pl.when(r > t)
+            def _():
+                tail_copy(1, k, t, left).wait_send()
+    for cond, copy in sends:
+        if cond is None:
+            copy.wait_send()
+        else:
+            @pl.when(cond)
+            def _():
+                copy.wait_send()
 
 
 def per_device(features, out_grad, weight, block_values, block_coords, block_counts):
@@ -246,11 +322,11 @@
     scale = 1.0 / math.sqrt(rows * R * C)
     vmem = pl.BlockSpec(memory_space=pltpu.VMEM)
     dma = pltpu.SemaphoreType.DMA
-    return pl.pallas_call(
-        functools.partial(kernel, R, C, scale),
+    activations, wsum, feature_grad = pl.pallas_call(
+        functools.partial(kernel, R, C),
         out_shape=(
             jax.ShapeDtypeStruct((rows, width), BF16),
-            jax.ShapeDtypeStruct((width, width), F32),
+            jax.ShapeDtypeStruct((width, width), BF16),
             jax.ShapeDtypeStruct((rows, width), BF16),
         ),
         in_specs=[pl.BlockSpec(memory_space=pltpu.SMEM), vmem, vmem, vmem, vmem],
@@ -267,8 +343,10 @@
             pltpu.VMEM((rows, width), F32),
             pltpu.VMEM((rows, width), BF16),
             pltpu.VMEM((K, C, rows, dc), BF16),
-            pltpu.VMEM((K, R, rows, dc), BF16),
-            pltpu.VMEM((K, R, rows, dc), BF16),
+            pltpu.VMEM((K, R, rows, dc), F32),
+            pltpu.VMEM((rows, dc), F32),
+            pltpu.VMEM((2, K, R, rows, dc), BF16),
+            pltpu.VMEM((2, K, R, rows, dc), BF16),
             pltpu.VMEM((C, part, width), F32),
             pltpu.VMEM((NC, part, width), BF16),
             pltpu.VMEM((NC, part, width), BF16),
@@ -276,12 +354,12 @@
             pltpu.VMEM((NC, part, width), BF16),
             pltpu.VMEM((R, part, width), BF16),
             pltpu.VMEM((C, part, width), BF16),
-            dma((K, R)), dma((K, R)),
+            dma((2, K, R)), dma((2, K, R)),
             dma((K,)), dma((K,)),
             dma((K, NC)), dma((K, NC)),
             dma((K, NC)), dma((K, NC)),
             dma((K, NC)), dma((K, NC)),
-            dma((K, R)), dma((K, R)),
+            dma((2, K, R)), dma((2, K, R)),
             dma, dma,
             dma((NC,)), dma((NC,)),
             dma((R,)), dma((R,)),
@@ -292,6 +370,7 @@
             collective_id=0, has_side_effects=True, vmem_limit_bytes=60 * 1024 * 1024
         ),
     )(slot_of, features, out_grad, weight, vals)
+    return activations, wsum.astype(F32) * F32(scale), feature_grad
 
 
 def solution(mesh):

time: 83.8 us -> 80.9 us (0.965)
  the two profiles are of different devices: /device:TPU:0 before, /device:TPU:9 now
where the time goes in v2:
time: 80.9 us; the launch traced here: 80.7 us
  Pallas kernels  71.4 us (88%)
  local copies, waits for them, and re-layouts  4.29 us (5%)
  other arithmetic  3.64 us (4%)
  between operations  1.3 us (2%)
    pallas_call x1, Pallas kernels, per_device(): pl.pallas_call(functools.partial(kernel, R, C), out_shape=(jax.ShapeDtype...  71.4 us
    reshape x1, local copies, waits for them, and re-layouts, per_device(): vals = block_values.reshape(slots, SIDE, SIDE)  2.92 us
    mul x1, other arithmetic, per_device(): return (activations, wsum.astype(F32) * F32(scale), feature_grad)  2.21 us

profile of v2, /device:TPU:9, one launch (start us, length us, event | category | flops | bytes accessed | tf_op | source)
XLA Modules:
  0.0 80.7 jit_solution(3183165529347226596)
XLA Ops:
  1.3 0.8 compare_select_fusion
  2.0 0.7 select_reduce_fusion.slot_ref
  2.7 2.9 %reshape.27.vals_ref = bf16[72,64,64]{2,1,0:T(8,128)(2,1)} reshape(bf16[1,1,72,4096]{3,2,1,0:T(8,128)(2,1)} %param.9) | data formatting | bytes 1179648 | tf_op jit(solution)/shard_map/reshape | solution.py:321
  5.6 71.4 %shard_map.85 = (bf16[192,512]{1,0:T(8,128)(2,1)}, bf16[512,512]{1,0:T(8,128)(2,1)}, bf16[192,512]{1,0:T(8,128)(2,1)}) custom-call(s32[288]{0:T(512)} %select_reduce_fusion.slot_ref, bf16[192,512]{1,0:T(8,128)(2,1)} %feat_ref.1, bf16[192,512]{1,0:T(8,128)(2,1)} %og_ref.1, bf16[512,512]{1,0:T(8,128)(2,1)} %w_ref.1, bf16[72,64,64]{2,1,0:T(8,128)(2,1)} %reshape.27.vals_ref), custom_call_target="tpu_custom_call" | custom-call | tf_op jit(solution)/shard_map/pallas_call | solution.py:325
  77.1 0.0 copy-start.1
  77.1 0.0 copy-start
  77.1 2.2 %convert_multiply_fusion = f32[512,512]{1,0:T(8,128)} fusion(bf16[512,512]{1,0:T(8,128)(2,1)} %get-tuple-element.7), kind=kLoop, calls=%fused_computation | loop fusion | flops 524288 | bytes 1572864 | tf_op jit(solution)/shard_map/mul | solution.py:373
  79.3 0.0 copy-done.1
  79.3 0.7 copy.12
  80.0 0.0 copy-done
  80.0 0.7 copy.13
Async XLA Ops:
  77.1 2.2 %copy-start.1 = (bf16[192,512]{1,0:T(8,128)(2,1)S(1)}, bf16[192,512]{1,0:T(8,128)(2,1)}, u32[]{:S(2)}) copy-start(bf16[192,512]{1,0:T(8,128)(2,1)} %get-tuple-element.12) | copy-start | bytes 589828
  77.1 2.9 %copy-start = (bf16[192,512]{1,0:T(8,128)(2,1)S(1)}, bf16[192,512]{1,0:T(8,128)(2,1)}, u32[]{:S(2)}) copy-start(bf16[192,512]{1,0:T(8,128)(2,1)} %get-tuple-element.14) | copy-start | bytes 589828
